TPU v7x, 256 devices: a whole 4x4x8 slice. The times are simulated.
256 devices in a mesh: blk: 16 (over z_hi, y), shard: 16 (over x, z_lo, core).
Axes of the slice: x: 4, y: 4, z: 8 (z_hi: 4, z_lo: 2; z = z_hi * 2 + z_lo), core: 2. Of those that a mesh axis runs over, the one named last changes fastest.
Arguments:
- picture_vectors: bfloat16 [65536, 1152], P(('blk', 'shard')), may hold values from -0.18 to 0.18
- sentence_vectors: bfloat16 [524288, 1152], P(('blk', 'shard')), may hold values from -0.18 to 0.18
- slot_picture_number: int32 [524288], P(('blk', 'shard')), may hold values from 0 to 256, as said below
- score_multiplier: float32 [], replicated, may hold values from 5 to 10
- score_offset: float32 [], replicated, may hold values from -3 to -1
Outputs:
- loss_rows: float32 [65536], P(('blk', 'shard'))
- grad_images: bfloat16 [65536, 1152], P(('blk', 'shard'))
- grad_captions: bfloat16 [524288, 1152], P(('blk', 'shard'))
Inputs may be any that keep to these rules, and one draw needn't show every extreme that they name: `slot_picture_number`: in each block of 128 slots of a text device for one owner, live slots come first, in nondecreasing image order, and the rest hold 256. Every image is named by 1 to 5 of its owner's slots. Each owner has one block of 128 live slots whenever 128 <= 256.
All inputs are finite; a program needn't handle non-finite values.
Results may differ from a plain program's by a relative error of at most 0.017.
Values may be sent and summed in bfloat16 or wider, within the bound.
A program may use at most 128 MiB of HBM per device.

v0:
```python
import jax
import jax.numpy as jnp
from jax import lax
from jax.sharding import PartitionSpec as P

EPS = 1e-06


def unit_rows(values):
    norms = jnp.sqrt(jnp.sum(values * values, axis=-1, keepdims=True) + EPS)
    return (values / norms, norms)


def oriented_match_scores(
    picture_group_matrix,
    sentence_group_matrix,
    picture_outer_dimension,
    score_multiplier,
    score_offset,
):
    match_scores = (
        score_multiplier
        * lax.dot_general(
            picture_group_matrix,
            sentence_group_matrix,
            (((1,), (1,)), ((), ())),
            preferred_element_type=jnp.float32,
        )
        + score_offset
    )
    image_ids = picture_outer_dimension + jnp.arange(picture_group_matrix.shape[0], dtype=jnp.int32)
    text_ids = jnp.arange(sentence_group_matrix.shape[0], dtype=jnp.int32)
    label_sign_table = jnp.where(image_ids[:, None] == text_ids[None, :], 1.0, -1.0).astype(
        jnp.float32
    )
    return (label_sign_table * match_scores, label_sign_table)


def pair_gradient(signed_logits, label_sign_table):
    return (-label_sign_table * jax.nn.sigmoid(-signed_logits)).astype(jnp.bfloat16)


def body(picture_vectors, sentence_vectors, slot_picture_number, score_multiplier, score_offset):
    image_count, feature_width = picture_vectors.shape
    column = image_count * lax.axis_size("blk")
    holder_outer_dimension = lax.axis_index("blk") * image_count
    received, received_ids = (
        lax.all_to_all(sentence_vectors, "shard", split_axis=0, concat_axis=0, tiled=True),
        lax.all_to_all(slot_picture_number, "shard", split_axis=0, concat_axis=0, tiled=True),
    )
    targets = jnp.arange(image_count, dtype=jnp.int32)
    onehot = (received_ids[None, :] == targets[:, None]).astype(jnp.bfloat16)
    summed = jnp.dot(onehot, received, preferred_element_type=jnp.float32)
    text_unit, text_norm = unit_rows(summed)
    text_half = text_unit.astype(jnp.bfloat16)
    image_unit, image_norm = unit_rows(picture_vectors.astype(jnp.float32))
    picture_vector_share = image_unit.astype(jnp.bfloat16)
    start_state = (
        jnp.zeros((image_count,), jnp.float32),
        jnp.zeros((image_count, feature_width), jnp.float32),
    )
    start_state = start_state + (jnp.zeros((image_count, column), jnp.bfloat16),)
    incomplete_share = lax.all_gather(text_half, "blk", axis=0, tiled=True)
    signed_logits, label_sign_table = oriented_match_scores(
        picture_vector_share,
        incomplete_share,
        holder_outer_dimension,
        score_multiplier,
        score_offset,
    )
    match_derivatives = pair_gradient(signed_logits, label_sign_table)
    losses = jnp.sum(-jax.nn.log_sigmoid(signed_logits), axis=1)
    picture_derivative = score_multiplier * jnp.dot(
        match_derivatives, incomplete_share, preferred_element_type=jnp.float32
    )
    folded = (losses, picture_derivative, match_derivatives)
    losses = folded[0]
    picture_derivative = folded[1]
    all_pairs = folded[2]
    text_grad = lax.psum_scatter(
        (
            score_multiplier
            * lax.dot_general(
                all_pairs,
                picture_vector_share,
                (((0,), (0,)), ((), ())),
                preferred_element_type=jnp.float32,
            )
        ).astype(jnp.bfloat16),
        "blk",
        scatter_dimension=0,
        tiled=True,
    ).astype(jnp.float32)
    grad_images = (
        (
            picture_derivative
            - image_unit * jnp.sum(image_unit * picture_derivative, axis=-1, keepdims=True)
        )
        / image_norm
    ).astype(jnp.bfloat16)
    pool_grad = (
        text_grad - text_unit * jnp.sum(text_unit * text_grad, axis=-1, keepdims=True)
    ) / text_norm
    scaled = pool_grad.astype(jnp.bfloat16)
    slot_grads = lax.dot_general(
        onehot, scaled, (((0,), (0,)), ((), ())), preferred_element_type=jnp.float32
    ).astype(jnp.bfloat16)
    grad_captions = lax.all_to_all(slot_grads, "shard", split_axis=0, concat_axis=0, tiled=True)
    return (losses / column, grad_images, grad_captions)


def solution(mesh):
    return jax.shard_map(
        body,
        mesh=mesh,
        in_specs=(
            P(("blk", "shard"), None),
            P(("blk", "shard"), None),
            P(("blk", "shard")),
            P(),
            P(),
        ),
        out_specs=(P(("blk", "shard")), P(("blk", "shard"), None), P(("blk", "shard"), None)),
        check_vma=False,
    )
```

profile of v0, /device:TPU:33, one launch (start us, length us, event | category | flops | bytes accessed | tf_op | source)
XLA Modules:
  0.0 432.2 jit_solution(839893366607783145)
XLA Ops:
  7.2 0.0 all-gather.2.cloned.1.call-start
  7.2 10.4 %all_to_all.33 = s32[16,128,1]{1,2,0:T(1,128)S(1)} all-to-all(s32[16,128,1]{1,2,0:T(1,128)} %bitcast.14), channel_id=1, replica_groups=mesh['blk'=16,'shard'=16] {'shard'}, dimensions={0} | all-to-all | bytes 16384 | tf_op jit(solution)/shard_map/all_to_all | solution.py:49
  17.6 60.0 %all_to_all.34 = bf16[16,128,1152]{2,1,0:T(8,128)(2,1)S(1)} all-to-all(bf16[16,128,1152]{2,1,0:T(8,128)(2,1)} %bitcast.11), channel_id=1, replica_groups=mesh['blk'=16,'shard'=16] {'shard'}, dimensions={0} | all-to-all | bytes 9437184 | tf_op jit(solution)/shard_map/all_to_all | solution.py:48
  77.6 0.0 copy-start
  77.6 1.7 multiply_reduce_fusion.1
  79.3 1.0 fusion.17
  80.3 0.0 all-gather.2.cloned.1.call-update
  80.3 0.0 reduce-scatter.2.cloned.1.call-start
  81.7 0.0 copy-done
  81.7 0.2 fusion.6
  81.9 126.2 %all-gather.2.cloned.1.call-done = bf16[4096,1152]{1,0:T(8,128)(2,1)} async-done(((bf16[256,1152]{1,0:T(8,128)(2,1)}), bf16[4096,1152]{1,0:T(8,128)(2,1)}) %all-gather.2.cloned.1.call-update) | async-done | bytes 9437200 | tf_op jit(solution)/shard_map/all_gather | solution.py:63
  208.1 7.7 %fusion.4 = (f32[256]{0:T(256)S(1)}, f32[256,4096]{1,0:T(8,128)S(1)}) fusion(f32[]{:T(128)S(6)} %copy.11, bf16[4096,1152]{1,0:T(8,128)(2,1)} %all-gather.2.cloned.1.call-done, f32[256]{0:T(256)S(1)} %add_sqrt_fusion.1, bf16[256,1152]{1,0:T(8,128)(2,1)S(1)} %copy-done, f32[]{:T(128)S(6)} %copy.10, s32[256]{0:T(256)S(1)} %iota_add_fusion), kind=kOutput, calls=%fused_computation.10 | convolution fusion | flops 2430435072 | bytes 14224392 | tf_op jit(solution)/shard_map/dot_general | solution.py:23
  215.8 0.0 copy-start.1
  215.8 2.0 copy-done.1
  217.8 6.3 %fusion = bf16[4096,1152]{1,0:T(8,128)(2,1)} fusion(f32[]{:T(128)S(6)} %copy.10, bf16[256,1152]{1,0:T(8,128)(2,1)S(1)} %copy-done, f32[256]{0:T(256)S(1)} %add_sqrt_fusion.1, f32[256,4096]{1,0:T(8,128)S(1)} %get-tuple-element.6, s32[256]{0:T(256)S(1)} %iota_add_fusion), kind=kOutput, calls=%fused_computation.1 | convolution fusion | flops 2433581056 | bytes 14223364 | tf_op jit(solution)/shard_map/dot_general | solution.py:83
  224.1 0.0 reduce-scatter.2.cloned.1.call-update
  224.2 128.5 %reduce-scatter.2.cloned.1.call-done = bf16[256,1152]{1,0:T(8,128)(2,1)} async-done(((bf16[4096,1152]{1,0:T(8,128)(2,1)}), bf16[256,1152]{1,0:T(8,128)(2,1)}) %reduce-scatter.2.cloned.1.call-update) | async-done | bytes 589840 | tf_op jit(solution)/shard_map/reduce_scatter | solution.py:80
  352.7 1.4 fusion.7
  354.1 5.2 %convolution_convert_fusion = bf16[2048,1152]{1,0:T(8,128)(2,1)} fusion(s32[2048]{0:T(1024)S(1)} %bitcast.16, bf16[256,1152]{1,0:T(8,128)(2,1)} %reduce-scatter.2.cloned.1.call-done, f32[256]{0:T(256)S(1)} %fusion.7, f32[256]{0:T(256)S(1)} %add_sqrt_fusion, f32[256,1152]{1,0:T(8,128)S(1)} %get-tuple-element.4), kind=kOutput, calls=%fused_computation.3 | convolution fusion | flops 1212612608 | bytes 6498304 | tf_op jit(solution)/shard_map/dot_general | solution.py:105
  359.3 6.3 %all-to-all-start.2 = ((bf16[16,128,1152]{2,1,0:T(8,128)(2,1)}), bf16[16,128,1152]{2,1,0:T(8,128)(2,1)}, u32[]{:S(2)}, u32[]{:S(2)}) async-start(bf16[16,128,1152]{2,1,0:T(8,128)(2,1)} %bitcast.12), calls=%async_computation.3 | async-start | bytes 9437184 | tf_op jit(solution)/shard_map/all_to_all | solution.py:108
  365.7 0.6 broadcast_multiply_fusion
  366.2 8.2 %multiply_reduce_fusion = (f32[256]{0:T(256)S(1)}, f32[256,1152]{1,0:T(8,128)S(1)}) fusion(f32[256]{0:T(256)S(1)} %add_sqrt_fusion.1, bf16[256,1152]{1,0:T(8,128)(2,1)S(1)} %copy-done, bf16[4096,1152]{1,0:T(8,128)(2,1)} %all-gather.2.cloned.1.call-done, f32[256,4096]{1,0:T(8,128)} %copy-done.1, s32[256]{0:T(256)S(1)} %iota_add_fusion, f32[]{:T(128)S(6)} %copy.10), kind=kOutput, calls=%fused_computation.24 | convolution fusion | flops 2424733440 | bytes 15404036 | tf_op jit(solution)/shard_map/dot_general | solution.py:73
  374.4 1.1 divide_convert_fusion
  375.5 45.0 %all-to-all-done.2 = bf16[16,128,1152]{2,1,0:T(8,128)(2,1)} async-done(((bf16[16,128,1152]{2,1,0:T(8,128)(2,1)}), bf16[16,128,1152]{2,1,0:T(8,128)(2,1)}, u32[]{:S(2)}, u32[]{:S(2)}) %all-to-all-start.2) | async-done | bytes 4718624 | tf_op jit(solution)/shard_map/all_to_all | solution.py:108
  420.5 4.9 %copy.12 = bf16[2048,1152]{1,0:T(8,128)(2,1)} copy(bf16[2048,1152]{1,0:T(8,128)(2,1)} %bitcast.6) | data formatting | bytes 9437184
  (3 shorter events, 0.0 us)
Async XLA Ops:
  7.2 200.9 %all-gather.2.cloned.1.call-start = ((), (), s32[]{:S(2)}) async-start(), calls=%async_computation.4 | async-start | bytes 10027008 | tf_op jit(solution)/shard_map/all_gather | solution.py:63
  77.6 4.1 copy-start
  80.3 272.3 %reduce-scatter.2.cloned.1.call-start = ((), (), s32[]{:S(2)}) async-start(), calls=%async_computation.5 | async-start | bytes 10027008 | tf_op jit(solution)/shard_map/reduce_scatter | solution.py:80
  215.8 2.0 copy-start.1
  359.3 61.1 %all-to-all-start.2 = ((bf16[16,128,1152]{2,1,0:T(8,128)(2,1)}), bf16[16,128,1152]{2,1,0:T(8,128)(2,1)}, u32[]{:S(2)}, u32[]{:S(2)}) async-start(bf16[16,128,1152]{2,1,0:T(8,128)(2,1)} %bitcast.12), calls=%async_computation.3 | async-start | bytes 9437184 | tf_op jit(solution)/shard_map/all_to_all | solution.py:108
Sparse Core Ops, SparseCore 0:
  80.5 127.5 all-gather.1
  224.3 128.3 reduce-scatter.1
where the time goes:
time: 434 us; the launch traced here: 432 us
  waiting for transfers between devices  300 us (69%)
  blocking collectives  70.4 us (16%)
  matrix products  29.1 us (7%)
  between operations  15.4 us (4%)
  local copies, waits for them, and re-layouts  6.91 us (2%)
  starting transfers between devices  6.43 us (1%)
    reduce_scatter x1, waiting for transfers between devices, body(): lax.psum_scatter((score_multiplier * lax.dot_general(all_pairs, picture_v...  129 us
    all_gather x1, waiting for transfers between devices, body(): incomplete_share = lax.all_gather(text_half, 'blk', axis=0, tiled=True)  126 us
    all_to_all x1, blocking collectives, body(): lax.all_to_all(sentence_vectors, 'shard', split_axis=0, concat_axis=0, ti...  60 us
    all_to_all x1, waiting for transfers between devices, body(): lax.all_to_all(slot_grads, 'shard', split_axis=0, concat_axis=0, tiled=True)  45 us
    all_to_all x1, blocking collectives, body(): lax.all_to_all(slot_picture_number, 'shard', split_axis=0, concat_axis=0,...  10.4 us
  transfers between devices with their start and end apart: 3, of which 3 were waited for; matrix products, arithmetic and copies ran while one was open for 2% of the time, Pallas kernels for 0%

commit v1 on v0

v1 whole, which is shorter than its diff:
```python
import jax
import jax.numpy as jnp
from jax import lax
from jax.experimental import pallas as pl
from jax.experimental.pallas import tpu as pltpu
from jax.sharding import PartitionSpec as P

EPS = 1e-06
D = 1152
ROWS = 256
SLOT = 128
NB = 16
TOTAL = NB * ROWS
F32 = jnp.float32
BF16 = jnp.bfloat16
CHUNK = 384
CHUNKS = D // CHUNK
N_COPY = 72


def pair_terms(scores, diagonal):
    u = jnp.where(diagonal, -scores, scores)
    e = jnp.exp(-jnp.abs(u))
    r = 1.0 / (1.0 + e)
    sig = jnp.where(u >= 0, r, e * r)
    return u, e, jnp.where(diagonal, -sig, sig)


def kernel(
    mult_ref,
    off_ref,
    ids_ref,
    img_ref,
    cap_ref,
    loss_ref,
    gimg_ref,
    gcap_ref,
    xr,
    idr,
    imgs,
    txts,
    psend,
    prec,
    hot,
    hot_t,
    g2,
    g1,
    tsum,
    tgrad,
    igrad,
    sc,
    gsend,
    grecv,
    lsend,
    lrecv,
    lown,
    send_sem,
    recv_sem,
    local_sem,
):
    g = lax.axis_index("blk")
    h = lax.axis_index("shard")
    zh, y = lax.div(g, 4), lax.rem(g, 4)
    x, w = lax.div(h, 4), lax.rem(h, 4)

    def ring(value, step):
        return lax.rem(value + step, 4)

    def at_x(step):
        return (g, ring(x, step) * 4 + w)

    def at_w(step):
        return (g, x * 4 + ring(w, step))

    def at_z(step):
        return (ring(zh, step) * 4 + y, h)

    def at_y(step):
        return (zh * 4 + ring(y, step), h)

    made = []
    local = []

    def send(src, dst, device):
        k = len(made)
        copy = pltpu.make_async_remote_copy(
            src_ref=src,
            dst_ref=dst,
            send_sem=send_sem.at[k],
            recv_sem=recv_sem.at[k],
            device_id=device,
            device_id_type=pl.DeviceIdType.MESH,
        )
        copy.start()
        made.append(copy)
        return copy

    def move(src, dst):
        copy = pltpu.make_async_copy(src, dst, local_sem.at[len(local)])
        copy.start()
        local.append(copy)
        return copy

    def rows(block, first=0, count=ROWS):
        return pl.ds(pl.multiple_of(block * ROWS + first, 128), count)

    def cols(j):
        return slice(j * CHUNK, (j + 1) * CHUNK)

    barrier = pltpu.get_barrier_semaphore()
    partners = [at_x(s) for s in (1, 2, 3)] + [at_w(s) for s in (1, 2, 3)]
    partners += [at_z(s) for s in (1, 3)] + [at_y(s) for s in (1, 2, 3)]
    for device in partners:
        pl.semaphore_signal(barrier, inc=1, device_id=device, device_id_type=pl.DeviceIdType.MESH)
    pl.semaphore_wait(barrier, len(partners))

    id_copies = [send(ids_ref.at[ring(x, s)], idr.at[x], at_x(s)) for s in (2, 1, 3)]
    id_own = move(ids_ref.at[x], idr.at[x])
    x_copies, x_own = [], []
    for j in range(CHUNKS):
        x_copies.append(
            [
                send(
                    cap_ref.at[pl.ds(pl.multiple_of(ring(x, s) * 512, 512), 512), cols(j)],
                    xr.at[x, :, cols(j)],
                    at_x(s),
                )
                for s in (2, 1, 3)
            ]
        )
        x_own.append(
            move(
                cap_ref.at[pl.ds(pl.multiple_of(x * 512, 512), 512), cols(j)], xr.at[x, :, cols(j)]
            )
        )

    pics = img_ref[...].astype(F32)
    pic_norm = jnp.sqrt(jnp.sum(pics * pics, axis=-1, keepdims=True) + EPS)
    imgs[rows(g), :] = (pics / pic_norm).astype(BF16)

    def start_y(step):
        block = ring(zh, step) * 4 + y
        piece = imgs.at[rows(block)]
        return [send(piece, piece, at_y(1)), send(piece, piece, at_y(3))]

    def forward_y(step, copies):
        up, down = copies
        up.wait_recv()
        piece = imgs.at[rows(ring(zh, step) * 4 + ring(y, 3), 0, 128)]
        first = send(piece, piece, at_y(1))
        down.wait_recv()
        piece = imgs.at[rows(ring(zh, step) * 4 + ring(y, 1), 128, 128)]
        return [first, send(piece, piece, at_y(3))]

    piece = imgs.at[rows(g)]
    z_copies = [send(piece, piece, at_z(1)), send(piece, piece, at_z(3))]
    y_first = {0: start_y(0)}
    y_halves = {0: forward_y(0, y_first[0])}

    z_copies[0].wait_recv()
    piece = imgs.at[rows(ring(zh, 3) * 4 + y, 0, 128)]
    z_halves = [send(piece, piece, at_z(1))]
    y_first[3] = start_y(3)
    z_copies[1].wait_recv()
    piece = imgs.at[rows(ring(zh, 1) * 4 + y, 128, 128)]
    z_halves.append(send(piece, piece, at_z(3)))
    y_first[1] = start_y(1)

    id_own.wait()
    for copy in id_copies:
        copy.wait_recv()
    image_rows = lax.broadcasted_iota(jnp.int32, (ROWS, SLOT), 0)
    for o in range(4):
        for s in range(4):
            table = (idr[s, o : o + 1, :] == image_rows).astype(F32)
            hot[o, :, s * SLOT : (s + 1) * SLOT] = table.astype(BF16)
            hot_t[o, s * SLOT : (s + 1) * SLOT, :] = table.T.astype(BF16)

    def pool(j):
        x_own[j].wait()
        for copy in x_copies[j]:
            copy.wait_recv()
        for o in range(4):
            stack = jnp.concatenate(
                [xr[s, o * SLOT : (o + 1) * SLOT, cols(j)] for s in range(4)], axis=0
            )
            psend[o, :, cols(j)] = jnp.dot(
                hot[o], stack, preferred_element_type=F32
            ).astype(BF16)
        return [
            send(psend.at[ring(w, s), :, cols(j)], prec.at[w, :, cols(j)], at_w(s))
            for s in (1, 2, 3)
        ]

    p_copies = [pool(0)]
    for copy in z_halves:
        copy.wait_recv()
    y_first[2] = start_y(2)
    y_halves[3] = forward_y(3, y_first[3])
    p_copies.append(pool(1))
    y_halves[1] = forward_y(1, y_first[1])
    p_copies.append(pool(2))
    y_halves[2] = forward_y(2, y_first[2])

    square = jnp.zeros((ROWS, 1), F32)
    for j in range(CHUNKS):
        for copy in p_copies[j]:
            copy.wait_recv()
        total = psend[w, :, cols(j)].astype(F32)
        for s in (1, 2, 3):
            total += prec[ring(w, s), :, cols(j)].astype(F32)
        tsum[:, cols(j)] = total
        square += jnp.sum(total * total, axis=-1, keepdims=True)
    text_norm = jnp.sqrt(square + EPS)
    unit = tsum[...] / text_norm
    tsum[...] = unit
    txts[rows(zh), :] = unit.astype(BF16)
    piece = txts.at[rows(zh)]
    t_copies = [send(piece, piece, at_z(1)), send(piece, piece, at_z(3))]

    mult, off = mult_ref[0], off_ref[0]
    gap = lax.broadcasted_iota(jnp.int32, (ROWS, ROWS), 0) - lax.broadcasted_iota(
        jnp.int32, (ROWS, ROWS), 1
    )
    nt = (((1,), (1,)), ((), ()))

    for step in (0, 3, 1, 2):
        for copy in y_halves[step]:
            copy.wait_recv()

        def text_block(k, carry, step=step):
            block = ring(zh, step) * 4 + k
            scores = lax.dot_general(
                txts[rows(zh), :], imgs[rows(block), :], nt, preferred_element_type=F32
            )
            diagonal = gap == jnp.where(block == g, 0, 2 * ROWS)
            terms = pair_terms(mult * scores + off, diagonal)
            g2[:, rows(block)] = terms[2].astype(BF16)
            return carry

        lax.fori_loop(0, 4, text_block, 0)

    for j in range(CHUNKS):
        tgrad[:, cols(j)] = mult * jnp.dot(
            g2[...], imgs[:, cols(j)], preferred_element_type=F32
        )

    t_copies[0].wait_recv()
    piece = txts.at[rows(ring(zh, 3), 0, 128)]
    t_halves = [send(piece, piece, at_z(1))]
    t_copies[1].wait_recv()
    piece = txts.at[rows(ring(zh, 1), 128, 128)]
    t_halves.append(send(piece, piece, at_z(3)))

    along = jnp.sum(tsum[...] * tgrad[...], axis=-1, keepdims=True)
    s_copies = []
    for j in range(CHUNKS):
        sc[w, :, cols(j)] = (
            (tgrad[:, cols(j)] - tsum[:, cols(j)] * along) / text_norm
        ).astype(BF16)
        s_copies.append(
            [send(sc.at[w, :, cols(j)], sc.at[w, :, cols(j)], at_w(s)) for s in (1, 2, 3)]
        )

    out_copies, out_own = [], []
    for j in range(CHUNKS):
        for copy in s_copies[j]:
            copy.wait_recv()
        for s in (2, 1, 3, 0):
            for o in range(4):
                xr[ring(x, s), o * SLOT : (o + 1) * SLOT, cols(j)] = jnp.dot(
                    hot_t[o, pl.ds(pl.multiple_of(ring(x, s) * SLOT, SLOT), SLOT), :],
                    sc[o, :, cols(j)],
                    preferred_element_type=F32,
                ).astype(BF16)
            src = xr.at[ring(x, s), :, cols(j)]
            dst = gcap_ref.at[pl.ds(pl.multiple_of(x * 512, 512), 512), cols(j)]
            if s:
                out_copies.append(send(src, dst, at_x(s)))
            else:
                out_own.append(move(src, dst))

    for copy in t_halves:
        copy.wait_recv()
    i_copies = []
    for step in (2, 1, 3, 0):
        block = zh * 4 + ring(y, step)
        loss_part = jnp.zeros((ROWS, 128), F32)
        for k in range(4):
            scores = lax.dot_general(
                imgs[rows(block), :],
                txts[k * ROWS : (k + 1) * ROWS, :],
                nt,
                preferred_element_type=F32,
            )
            if step:
                diagonal = jnp.zeros((ROWS, ROWS), jnp.bool_)
            else:
                diagonal = gap == jnp.where(zh == k, 0, 2 * ROWS)
            u, e, grad = pair_terms(mult * scores + off, diagonal)
            losses = jnp.maximum(u, 0.0) + jnp.log1p(e)
            loss_part += losses[:, :128] + losses[:, 128:]
            g1[:, k * ROWS : (k + 1) * ROWS] = grad.astype(BF16)
        part = mult * jnp.dot(g1[...], txts[...], preferred_element_type=F32)
        if step:
            gsend[step - 1] = part.astype(BF16)
            lsend[step - 1] = loss_part
            i_copies.append(send(gsend.at[step - 1], grecv.at[step - 1], at_y(step)))
            i_copies.append(send(lsend.at[step - 1], lrecv.at[step - 1], at_y(step)))
        else:
            igrad[...] = part
            lown[...] = loss_part
    for copy in i_copies:
        copy.wait_recv()

    losses = lown[...] + lrecv[0] + lrecv[1] + lrecv[2]
    loss_ref[...] = jnp.sum(losses.T, axis=0, keepdims=True) / TOTAL
    total = igrad[...]
    for s in range(3):
        total += grecv[s].astype(F32)
    pics = img_ref[...].astype(F32)
    pic_norm = jnp.sqrt(jnp.sum(pics * pics, axis=-1, keepdims=True) + EPS)
    unit = pics / pic_norm
    along = jnp.sum(unit * total, axis=-1, keepdims=True)
    gimg_ref[...] = ((total - unit * along) / pic_norm).astype(BF16)

    for copy in out_copies:
        copy.wait_recv()
    for copy in out_own:
        copy.wait()
    for copy in made:
        copy.wait_send()


def body(picture_vectors, sentence_vectors, slot_picture_number, score_multiplier, score_offset):
    vmem = pl.BlockSpec(memory_space=pltpu.VMEM)
    smem = pl.BlockSpec(memory_space=pltpu.SMEM)
    anywhere = pl.BlockSpec(memory_space=pl.ANY)
    loss, grad_images, grad_captions = pl.pallas_call(
        kernel,
        out_shape=(
            jax.ShapeDtypeStruct((1, ROWS), F32),
            jax.ShapeDtypeStruct((ROWS, D), BF16),
            jax.ShapeDtypeStruct((16 * SLOT, D), BF16),
        ),
        in_specs=[smem, smem, vmem, vmem, anywhere],
        out_specs=(vmem, vmem, anywhere),
        scratch_shapes=[
            pltpu.VMEM((4, 512, D), BF16),
            pltpu.VMEM((4, 4, SLOT), jnp.int32),
            pltpu.VMEM((TOTAL, D), BF16),
            pltpu.VMEM((4 * ROWS, D), BF16),
            pltpu.VMEM((4, ROWS, D), BF16),
            pltpu.VMEM((4, ROWS, D), BF16),
            pltpu.VMEM((4, ROWS, 4 * SLOT), BF16),
            pltpu.VMEM((4, 4 * SLOT, ROWS), BF16),
            pltpu.VMEM((ROWS, TOTAL), BF16),
            pltpu.VMEM((ROWS, 4 * ROWS), BF16),
            pltpu.VMEM((ROWS, D), F32),
            pltpu.VMEM((ROWS, D), F32),
            pltpu.VMEM((ROWS, D), F32),
            pltpu.VMEM((4, ROWS, D), BF16),
            pltpu.VMEM((3, ROWS, D), BF16),
            pltpu.VMEM((3, ROWS, D), BF16),
            pltpu.VMEM((3, ROWS, 128), F32),
            pltpu.VMEM((3, ROWS, 128), F32),
            pltpu.VMEM((ROWS, 128), F32),
            pltpu.SemaphoreType.DMA((N_COPY,)),
            pltpu.SemaphoreType.DMA((N_COPY,)),
            pltpu.SemaphoreType.DMA((8,)),
        ],
        compiler_params=pltpu.CompilerParams(
            collective_id=0, has_side_effects=True, vmem_limit_bytes=56 * 1024 * 1024
        ),
        cost_estimate=pl.CostEstimate(
            flops=13_000_000_000, bytes_accessed=12_000_000, transcendentals=4_000_000
        ),
        name="pooled_sigmoid_loss",
    )(
        score_multiplier.reshape(1),
        score_offset.reshape(1),
        slot_picture_number.reshape(4, 4, SLOT),
        picture_vectors,
        sentence_vectors,
    )
    return loss.reshape(ROWS), grad_images, grad_captions


def solution(mesh):
    return jax.shard_map(
        body,
        mesh=mesh,
        in_specs=(
            P(("blk", "shard"), None),
            P(("blk", "shard"), None),
            P(("blk", "shard")),
            P(),
            P(),
        ),
        out_specs=(P(("blk", "shard")), P(("blk", "shard"), None), P(("blk", "shard"), None)),
        check_vma=False,
    )
```

time: 434 us -> 197 us (0.45)
  waiting for transfers between devices: 300 us -> 0 us
  Pallas kernels: 0 us -> 186 us
  blocking collectives: 70.4 us -> 0 us
  matrix products: 29.1 us -> 0 us
  between operations: 15.4 us -> 1.93 us
  starting transfers between devices: 6.43 us -> 0 us
    pallas_call x0 -> x1, Pallas kernels: none -> 186 us  [body(): pl.pallas_call(kernel, out_shape=(jax.ShapeDtypeStruct((1, ROWS), F32), j...]
    reduce_scatter x1 -> x0, waiting for transfers between devices: 129 us -> none  [body(): lax.psum_scatter((score_multiplier * lax.dot_general(all_pairs, picture_v...]
    all_gather x1 -> x0, waiting for transfers between devices: 126 us -> none  [body(): incomplete_share = lax.all_gather(text_half, 'blk', axis=0, tiled=True)]
    all_to_all x2 -> x0, blocking collectives: 70.4 us -> none  [the longest x1 60 us: body(): lax.all_to_all(sentence_vectors, 'shard', split_axis=0, concat_axis=0, ti...]
    all_to_all x1 -> x0, waiting for transfers between devices: 45 us -> none  [body(): lax.all_to_all(slot_grads, 'shard', split_axis=0, concat_axis=0, tiled=True)]
    dot_general x5 -> x0, matrix products: 29.1 us -> none  [the longest x1 8.16 us: body(): jnp.dot(match_derivatives, incomplete_share, preferred_element_type=jnp.f...]
    all_to_all x1 -> x0, starting transfers between devices: 6.35 us -> none  [body(): lax.all_to_all(slot_grads, 'shard', split_axis=0, concat_axis=0, tiled=True)]
  transfers between devices with their start and end apart: 3 -> 0, of which waited for: 3 -> 0; matrix products, arithmetic and copies ran while one was open for 2% -> 0% of each run, Pallas kernels for 0% -> 0%
where the time goes in v1:
time: 197 us; the launch traced here: 196 us
  Pallas kernels  186 us (94%)
  local copies, waits for them, and re-layouts  8.02 us (4%)
    pallas_call x1, Pallas kernels, body(): pl.pallas_call(kernel, out_shape=(jax.ShapeDtypeStruct((1, ROWS), F32), j...  186 us
    unnamed x3, local copies, waits for them, and re-layouts  8.02 us

profile of v1, /device:TPU:33, one launch (start us, length us, event | category | flops | bytes accessed | tf_op | source)
XLA Modules:
  0.0 196.4 jit_solution(10328201678429936775)
XLA Ops:
  1.9 186.5 %pooled_sigmoid_loss.1 = (f32[1,256]{1,0:T(1,128)}, bf16[256,1152]{1,0:T(8,128)(2,1)}, bf16[2048,1152]{1,0:T(8,128)(2,1)}) custom-call(f32[1]{0:T(128)} %bitcast.4.mult_ref, f32[1]{0:T(128)} %bitcast.5.off_ref, s32[4,4,128]{2,1,0:T(4,128)} %bitcast.7, bf16[256,1152]{1,0:T(8,128)(2,1)} %img_ref.1, bf16[2048,1152]{1,0:T(8,128)(2,1)} %cap_ref.1), custom_call_target="tpu_custom_call" | custom-call | flops 12999999488 | bytes 12000000 | tf_op jit(solution)/shard_map/pooled_sigmoid_loss/pallas_call | solution.py:339
  188.4 1.2 copy.13
  189.6 1.9 copy.14
  191.5 4.9 %copy.15 = bf16[2048,1152]{1,0:T(8,128)(2,1)} copy(bf16[2048,1152]{1,0:T(8,128)(2,1)} %get-tuple-element.14) | data formatting | bytes 9437184

commit v2 on v1

v2 whole, which is shorter than its diff:
```python
import jax
import jax.numpy as jnp
from jax import lax
from jax.experimental import pallas as pl
from jax.experimental.pallas import tpu as pltpu
from jax.sharding import PartitionSpec as P

EPS = 1e-06
D = 1152
ROWS = 256
SLOT = 128
NB = 16
TOTAL = NB * ROWS
F32 = jnp.float32
BF16 = jnp.bfloat16
WIDTHS_IN = (384, 384, 256, 128)
WIDTHS_OUT = (128, 256, 384, 384)
N_COPY = 88


def spans(widths):
    starts = [sum(widths[:i]) for i in range(len(widths))]
    return [slice(s, s + n) for s, n in zip(starts, widths)]


IN, OUT = spans(WIDTHS_IN), spans(WIDTHS_OUT)


class Copy:
    def __init__(self, copy, when):
        self.copy, self.when = copy, when

    def act(self, step):
        if self.when is None:
            step()
        else:
            pl.when(self.when)(step)

    def wait_recv(self):
        self.act(self.copy.wait_recv)

    def wait_send(self):
        self.act(self.copy.wait_send)


def pair_gradient(scores, diagonal):
    u = jnp.where(diagonal, -scores, scores)
    sig = 1.0 / (1.0 + jnp.exp(-u))
    return jnp.where(diagonal, -sig, sig)


def pair_loss(scores, diagonal):
    u = jnp.where(diagonal, -scores, scores)
    return jnp.maximum(u, 0.0) + jnp.log1p(jnp.exp(-jnp.abs(u)))


def kernel(
    mult_ref,
    off_ref,
    ids_ref,
    img_ref,
    cap_ref,
    loss_ref,
    gimg_ref,
    gcap_ref,
    xr,
    idr,
    imgs,
    txts,
    psib,
    prsib,
    psend,
    prec,
    hot,
    hot_t,
    g2,
    g1,
    tsum,
    tgrad,
    tswap,
    sc,
    gsend,
    grecv,
    lsend,
    lrecv,
    send_sem,
    recv_sem,
    local_sem,
):
    g = lax.axis_index("blk")
    h = lax.axis_index("shard")
    zh, y = lax.div(g, 4), lax.rem(g, 4)
    x, w = lax.div(h, 4), lax.rem(h, 4)
    za, zb = lax.div(zh, 2), lax.rem(zh, 2)
    zl, b = lax.div(w, 2), lax.rem(w, 2)
    on = zb == b
    off = zb != b

    def ring(value, step):
        return lax.rem(value + step, 4)

    def at_x(step):
        return (g, ring(x, step) * 4 + w)

    def at_y(step):
        return (zh * 4 + ring(y, step), h)

    core = (g, x * 4 + zl * 2 + 1 - b)
    flipped = x * 4 + zl * 2 + 1 - b
    up = (jnp.where(on, ring(zh, 2), ring(zh, 1)) * 4 + y, jnp.where(on, h, flipped))
    down = (ring(zh, 3) * 4 + y, flipped)

    def partner(step):
        z = jnp.where(on, zh, za * 2 + 1 - zb)
        c = jnp.where(on, b, 1 - b)
        return (z * 4 + y, x * 4 + (1 - zl if step else zl) * 2 + c)

    made = []
    local = []

    def send(src, dst, device, when=None, start=True):
        k = len(made)
        copy = pltpu.make_async_remote_copy(
            src_ref=src,
            dst_ref=dst,
            send_sem=send_sem.at[k],
            recv_sem=recv_sem.at[k],
            device_id=device,
            device_id_type=pl.DeviceIdType.MESH,
        )
        made.append(Copy(copy, when))
        if start:
            made[-1].act(copy.start)
        return made[-1]

    def move(src, dst):
        copy = pltpu.make_async_copy(src, dst, local_sem.at[len(local)])
        copy.start()
        local.append(copy)
        return copy

    def rows(block, first=0, count=ROWS):
        return pl.ds(pl.multiple_of(block * ROWS + first, 128), count)

    def piece(owner):
        return pl.ds(pl.multiple_of(owner * 512, 512), 512)

    barrier = pltpu.get_barrier_semaphore()

    def greet(device):
        pl.semaphore_signal(barrier, inc=1, device_id=device, device_id_type=pl.DeviceIdType.MESH)

    partners = [at_x(s) for s in (1, 2, 3)] + [at_y(s) for s in (1, 3)]
    partners += [core, up, partner(1)]
    for device in partners:
        greet(device)

    @pl.when(off)
    def _():
        for device in (down, partner(0)):
            greet(device)

    pl.semaphore_wait(barrier, len(partners) + jnp.where(on, 0, 2))

    id_copies = [send(ids_ref.at[ring(x, s)], idr.at[x], at_x(s)) for s in (2, 1, 3)]
    id_own = move(ids_ref.at[x], idr.at[x])
    x_copies, x_own = [], []
    for span in IN:
        x_copies.append(
            [
                send(cap_ref.at[piece(ring(x, s)), span], xr.at[x, :, span], at_x(s))
                for s in (2, 1, 3)
            ]
        )
        x_own.append(move(cap_ref.at[piece(x), span], xr.at[x, :, span]))

    pics = img_ref[...].astype(F32)
    pic_norm = jnp.sqrt(jnp.sum(pics * pics, axis=-1, keepdims=True) + EPS)
    imgs[rows(y), :] = (pics / pic_norm).astype(BF16)
    first = jnp.where(on, 0, 4)
    z_near = jnp.where(on, zh, ring(zh, 3))
    z_far = jnp.where(on, ring(zh, 2), ring(zh, 1))

    def round_y(buffer, slot, start=True):
        src = buffer.at[rows(slot(y))]
        return [send(src, src, at_y(s), start=start) for s in (1, 3)]

    def pass_y(buffer, slot, copies, step):
        copies[0 if step == 3 else 1].wait_recv()
        src = buffer.at[rows(slot(ring(y, step)), 0 if step == 3 else 128, 128)]
        return send(src, src, at_y(4 - step))

    def near_slot(k):
        return first + k

    def far_slot(k):
        return first + 4 + k

    def text_slot(k):
        return k * 2 + b

    src = imgs.at[rows(y)]
    up_copy = send(src, imgs.at[rows(4 + y)], up)
    down_copy = send(src, imgs.at[rows(8 + y)], down, when=off)
    near = round_y(imgs, near_slot, start=False)
    far = round_y(imgs, far_slot, start=False)

    @pl.when(on)
    def _():
        for copy in near:
            copy.copy.start()

    id_own.wait()
    for copy in id_copies:
        copy.wait_recv()
    image_rows = lax.broadcasted_iota(jnp.int32, (ROWS, SLOT), 0)
    for o in range(4):
        for s in range(4):
            table = (idr[s, o : o + 1, :] == image_rows).astype(F32)
            hot[o, :, s * SLOT : (s + 1) * SLOT] = table.astype(BF16)
            hot_t[o, s * SLOT : (s + 1) * SLOT, :] = table.T.astype(BF16)

    up_copy.wait_recv()

    @pl.when(on)
    def _():
        for copy in far:
            copy.copy.start()

    @pl.when(off)
    def _():
        for copy in near:
            copy.copy.start()

    down_copy.wait_recv()

    @pl.when(off)
    def _():
        for copy in far:
            copy.copy.start()

    p_copies = []

    def pooled(owner, span):
        block = pl.ds(pl.multiple_of(owner * SLOT, SLOT), SLOT)
        stack = jnp.concatenate([xr[s, block, span] for s in range(4)], axis=0)
        return jnp.dot(hot[owner], stack, preferred_element_type=F32)

    def pool(j):
        span = IN[j]
        x_own[j].wait()
        for copy in x_copies[j]:
            copy.wait_recv()
        for t in range(2):
            psib[t, :, span] = pooled(t * 2 + 1 - b, span).astype(BF16)
        sib = send(psib.at[:, :, span], prsib.at[:, :, span], core)
        sums = [pooled(t * 2 + b, span) for t in range(2)]
        sib.wait_recv()
        for t in range(2):
            psend[t, :, span] = (sums[t] + prsib[t, :, span].astype(F32)).astype(BF16)
        p_copies.append(
            [
                send(psend.at[1 - zl, :, span], prec.at[1, :, span], partner(1)),
                send(psend.at[zl, :, span], prec.at[0, :, span], partner(0), when=off),
            ]
        )

        @pl.when(on)
        def _():
            prec[0, :, span] = psend[zl, :, span]

    pool(0)
    halves = [pass_y(imgs, near_slot, near, step) for step in (3, 1)]
    pool(1)
    halves += [pass_y(imgs, far_slot, far, step) for step in (3, 1)]
    for j in range(2, len(IN)):
        pool(j)

    square = jnp.zeros((ROWS, 1), F32)
    for j, span in enumerate(IN):
        for copy in p_copies[j]:
            copy.wait_recv()
        total = prec[0, :, span].astype(F32) + prec[1, :, span].astype(F32)
        tsum[:, span] = total
        square += jnp.sum(total * total, axis=-1, keepdims=True)
    text_scale = lax.rsqrt(square + EPS)
    unit = tsum[...] * text_scale
    tsum[...] = unit
    txts[rows(text_slot(y)), :] = unit.astype(BF16)
    src = txts.at[rows(text_slot(y))]
    t_swaps = [send(src, src, core)]
    t_copies = round_y(txts, text_slot)

    mult, offset = mult_ref[0], off_ref[0]
    gap = lax.broadcasted_iota(jnp.int32, (ROWS, ROWS), 0) - lax.broadcasted_iota(
        jnp.int32, (ROWS, ROWS), 1
    )
    nt = (((1,), (1,)), ((), ()))
    def diagonal(same):
        return gap == jnp.where(same, 0, 2 * ROWS)

    for copy in halves:
        copy.wait_recv()
    t_swaps[0].wait_recv()
    both = pl.ds(pl.multiple_of(y * 2 * ROWS, 128), 2 * ROWS)
    for k in range(8):
        scores = lax.dot_general(
            txts[both, :], imgs[rows(first + k), :], nt, preferred_element_type=F32
        )
        image_z = z_far if k // 4 else z_near
        for t in range(2):
            same = (y == k % 4) & (image_z == za * 2 + t)
            block = slice(t * ROWS, (t + 1) * ROWS)
            grad = pair_gradient(mult * scores[block] + offset, diagonal(same))
            g2[block, k * ROWS : (k + 1) * ROWS] = grad.astype(BF16)
    parts = (slice(0, 512), slice(512, 1024), slice(1024, D))
    g_swaps = []
    for span in parts:
        tgrad[:, span] = mult * jnp.dot(
            g2[...],
            imgs[pl.ds(pl.multiple_of(first * ROWS, 128), 8 * ROWS), span],
            preferred_element_type=F32,
        )
        tswap[0, :, span] = tgrad[rows(1 - b), span].astype(BF16)
        g_swaps.append(send(tswap.at[0, :, span], tswap.at[1, :, span], core))

    along = jnp.zeros((ROWS, 1), F32)
    for copy, span in zip(g_swaps, parts):
        copy.wait_recv()
        total = tgrad[rows(b), span] + tswap[1, :, span].astype(F32)
        tgrad[rows(b), span] = total
        along += jnp.sum(tsum[:, span] * total, axis=-1, keepdims=True)
    s_copies = []
    for span in OUT:
        tswap[2, :, span] = (
            (tgrad[rows(b), span] - tsum[:, span] * along) * text_scale
        ).astype(BF16)
        src = tswap.at[2, :, span]
        s_copies.append(
            [
                send(src, sc.at[zb * 2 + zl, :, span], partner(1)),
                send(src, sc.at[zb * 2 + zl, :, span], partner(0), when=off),
            ]
        )

        @pl.when(on)
        def _():
            sc[zb * 2 + zl, :, span] = tswap[2, :, span]

    out_copies, out_own = [], []
    t_halves = []
    for j, span in enumerate(OUT):
        for copy in s_copies[j]:
            copy.wait_recv()
        src = sc.at[pl.ds(b * 2, 2), :, span]
        send(src, src, core).wait_recv()
        for s in (2, 1, 3, 0):
            for o in range(4):
                xr[ring(x, s), o * SLOT : (o + 1) * SLOT, span] = jnp.dot(
                    hot_t[o, pl.ds(pl.multiple_of(ring(x, s) * SLOT, SLOT), SLOT), :],
                    sc[o % 2 * 2 + o // 2, :, span],
                    preferred_element_type=F32,
                ).astype(BF16)
            src = xr.at[ring(x, s), :, span]
            dst = gcap_ref.at[piece(x), span]
            if s:
                out_copies.append(send(src, dst, at_x(s)))
            else:
                out_own.append(move(src, dst))
        if j == 1:
            t_halves = [pass_y(txts, text_slot, t_copies, step) for step in (3, 1)]
            for step in (3, 1):
                src = txts.at[rows(text_slot(ring(y, step)))]
                t_swaps.append(send(src, src, core))

    for copy in t_halves:
        copy.wait_recv()
    src = txts.at[rows(text_slot(ring(y, 2)))]
    t_swaps.append(send(src, src, core))
    for copy in t_swaps[1:]:
        copy.wait_recv()
    i_copies = []
    for far in (1, 0):
        image_z = z_far if far else z_near
        loss_part = jnp.zeros((ROWS, 128), F32)
        for k in range(8):
            scores = lax.dot_general(
                imgs[rows(first + far * 4 + y), :],
                txts[k * ROWS : (k + 1) * ROWS, :],
                nt,
                preferred_element_type=F32,
            )
            same = (y == k // 2) & (image_z == za * 2 + k % 2)
            scores = mult * scores + offset
            grad = pair_gradient(scores, diagonal(same))
            losses = pair_loss(scores, diagonal(same))
            loss_part += losses[:, :128] + losses[:, 128:]
            g1[:, k * ROWS : (k + 1) * ROWS] = grad.astype(BF16)
        gsend[far] = (
            mult * jnp.dot(g1[...], txts[...], preferred_element_type=F32)
        ).astype(BF16)
        lsend[far] = loss_part
        device, when = (up, None) if far else (down, off)
        i_copies.append(send(gsend.at[far], grecv.at[far], device, when))
        i_copies.append(send(lsend.at[far], lrecv.at[far], device, when))

    @pl.when(on)
    def _():
        grecv[0] = gsend[0]
        lrecv[0] = lsend[0]

    for copy in i_copies:
        copy.wait_recv()

    losses = lrecv[0] + lrecv[1]
    loss_ref[...] = jnp.sum(losses.T, axis=0, keepdims=True) / TOTAL
    total = grecv[0].astype(F32) + grecv[1].astype(F32)
    pics = img_ref[...].astype(F32)
    pic_norm = jnp.sqrt(jnp.sum(pics * pics, axis=-1, keepdims=True) + EPS)
    unit = pics / pic_norm
    along = jnp.sum(unit * total, axis=-1, keepdims=True)
    gimg_ref[...] = ((total - unit * along) / pic_norm).astype(BF16)

    for copy in out_copies:
        copy.wait_recv()
    for copy in out_own:
        copy.wait()
    for copy in made:
        copy.wait_send()


def hand_over(loss_ref, gimg_ref, gcap_ref, loss_out, gimg_out, gcap_out, held, in_sem, out_sem):
    pieces = [(gcap_ref, gcap_out, i * ROWS) for i in range(8)] + [(gimg_ref, gimg_out, 0)]
    ins, outs = [], []
    for i, (src, dst, row) in enumerate(pieces):
        part = pl.ds(row, ROWS)
        ins.append(pltpu.make_async_copy(src.at[part], held.at[i], in_sem.at[i]))
        outs.append(pltpu.make_async_copy(held.at[i], dst.at[part], out_sem.at[i]))
        ins[i].start()
    for i in range(len(pieces)):
        ins[i].wait()
        outs[i].start()
    loss_out[...] = loss_ref[...]
    for copy in outs:
        copy.wait()


def body(picture_vectors, sentence_vectors, slot_picture_number, score_multiplier, score_offset):
    vmem = pl.BlockSpec(memory_space=pltpu.VMEM)
    smem = pl.BlockSpec(memory_space=pltpu.SMEM)
    anywhere = pl.BlockSpec(memory_space=pl.ANY)
    parts = pl.pallas_call(
        kernel,
        out_shape=(
            jax.ShapeDtypeStruct((1, ROWS), F32),
            jax.ShapeDtypeStruct((ROWS, D), BF16),
            jax.ShapeDtypeStruct((16 * SLOT, D), BF16),
        ),
        in_specs=[smem, smem, vmem, vmem, anywhere],
        out_specs=(vmem, vmem, anywhere),
        scratch_shapes=[
            pltpu.VMEM((4, 512, D), BF16),
            pltpu.VMEM((4, 4, SLOT), jnp.int32),
            pltpu.VMEM((12 * ROWS, D), BF16),
            pltpu.VMEM((8 * ROWS, D), BF16),
            pltpu.VMEM((2, ROWS, D), BF16),
            pltpu.VMEM((2, ROWS, D), BF16),
            pltpu.VMEM((2, ROWS, D), BF16),
            pltpu.VMEM((2, ROWS, D), BF16),
            pltpu.VMEM((4, ROWS, 4 * SLOT), BF16),
            pltpu.VMEM((4, 4 * SLOT, ROWS), BF16),
            pltpu.VMEM((2 * ROWS, 8 * ROWS), BF16),
            pltpu.VMEM((ROWS, 8 * ROWS), BF16),
            pltpu.VMEM((ROWS, D), F32),
            pltpu.VMEM((2 * ROWS, D), F32),
            pltpu.VMEM((3, ROWS, D), BF16),
            pltpu.VMEM((4, ROWS, D), BF16),
            pltpu.VMEM((2, ROWS, D), BF16),
            pltpu.VMEM((2, ROWS, D), BF16),
            pltpu.VMEM((2, ROWS, 128), F32),
            pltpu.VMEM((2, ROWS, 128), F32),
            pltpu.SemaphoreType.DMA((N_COPY,)),
            pltpu.SemaphoreType.DMA((N_COPY,)),
            pltpu.SemaphoreType.DMA((16,)),
        ],
        compiler_params=pltpu.CompilerParams(
            collective_id=0, has_side_effects=True, vmem_limit_bytes=56 * 1024 * 1024
        ),
        cost_estimate=pl.CostEstimate(
            flops=13_000_000_000, bytes_accessed=12_000_000, transcendentals=4_000_000
        ),
        name="pooled_sigmoid_loss",
    )(
        score_multiplier.reshape(1),
        score_offset.reshape(1),
        slot_picture_number.reshape(4, 4, SLOT),
        picture_vectors,
        sentence_vectors,
    )
    loss, grad_images, grad_captions = pl.pallas_call(
        hand_over,
        out_shape=tuple(jax.ShapeDtypeStruct(p.shape, p.dtype) for p in parts),
        in_specs=[vmem, anywhere, anywhere],
        out_specs=(vmem, anywhere, anywhere),
        scratch_shapes=[
            pltpu.VMEM((9, ROWS, D), BF16),
            pltpu.SemaphoreType.DMA((9,)),
            pltpu.SemaphoreType.DMA((9,)),
        ],
        compiler_params=pltpu.CompilerParams(vmem_limit_bytes=60 * 1024 * 1024),
        name="hand_over",
    )(*parts)
    return loss.reshape(ROWS), grad_images, grad_captions


def solution(mesh):
    return jax.shard_map(
        body,
        mesh=mesh,
        in_specs=(
            P(("blk", "shard"), None),
            P(("blk", "shard"), None),
            P(("blk", "shard")),
            P(),
            P(),
        ),
        out_specs=(P(("blk", "shard")), P(("blk", "shard"), None), P(("blk", "shard"), None)),
        check_vma=False,
    )
```

time: 197 us -> 162 us (0.82)
  Pallas kernels: 186 us -> 160 us
  local copies, waits for them, and re-layouts: 8.02 us -> 0 us
    pallas_call x1, Pallas kernels: 186 us -> 154 us  [body(): pl.pallas_call(kernel, out_shape=(jax.ShapeDtypeStruct((1, ROWS), F32), j...]
    unnamed x3 -> x0, local copies, waits for them, and re-layouts: 8.02 us -> none
    pallas_call x0 -> x1, Pallas kernels: none -> 5.97 us  [body(): pl.pallas_call(hand_over, out_shape=tuple((jax.ShapeDtypeStruct(p.shape,...]
where the time goes in v2:
time: 162 us
  Pallas kernels  160 us (99%)
  between operations  2.09 us (1%)
    pallas_call x1, Pallas kernels, body(): pl.pallas_call(kernel, out_shape=(jax.ShapeDtypeStruct((1, ROWS), F32), j...  154 us
    pallas_call x1, Pallas kernels, body(): pl.pallas_call(hand_over, out_shape=tuple((jax.ShapeDtypeStruct(p.shape,...  5.97 us

profile of v2, /device:TPU:33, one launch (start us, length us, event | category | flops | bytes accessed | tf_op | source)
XLA Modules:
  0.0 161.6 jit_solution(8300939555536459060)
XLA Ops:
  1.9 153.6 %pooled_sigmoid_loss.1 = (f32[1,256]{1,0:T(1,128)}, bf16[256,1152]{1,0:T(8,128)(2,1)}, bf16[2048,1152]{1,0:T(8,128)(2,1)}) custom-call(f32[1]{0:T(128)} %bitcast.4.mult_ref, f32[1]{0:T(128)} %bitcast.5.off_ref, s32[4,4,128]{2,1,0:T(4,128)} %bitcast.6, bf16[256,1152]{1,0:T(8,128)(2,1)} %img_ref.1, bf16[2048,1152]{1,0:T(8,128)(2,1)} %cap_ref.1), custom_call_target="tpu_custom_call" | custom-call | flops 12999999488 | bytes 12000000 | tf_op jit(solution)/shard_map/pooled_sigmoid_loss/pallas_call | solution.py:452
  155.5 6.0 %hand_over.1 = (f32[1,256]{1,0:T(1,128)}, bf16[256,1152]{1,0:T(8,128)(2,1)}, bf16[2048,1152]{1,0:T(8,128)(2,1)}) custom-call(f32[1,256]{1,0:T(1,128)} %get-tuple-element.9.loss_ref, bf16[256,1152]{1,0:T(8,128)(2,1)} %get-tuple-element.10.gimg_ref, bf16[2048,1152]{1,0:T(8,128)(2,1)} %get-tuple-element.11.gcap_ref), custom_call_target="tpu_custom_call" | custom-call | tf_op jit(solution)/shard_map/hand_over/pallas_call | solution.py:500

commit v3 on v2

--- a/solution.py
+++ b/solution.py
@@ -14,8 +14,8 @@
 F32 = jnp.float32
 BF16 = jnp.bfloat16
 WIDTHS_IN = (384, 384, 256, 128)
-WIDTHS_OUT = (128, 256, 384, 384)
-N_COPY = 88
+WIDTHS_OUT = (128, 256, 256, 256, 256)
+N_COPY = 112
 
 
 def spans(widths):
@@ -43,15 +43,21 @@
         self.act(self.copy.wait_send)
 
 
+def signed(scores, diagonal):
+    return scores if diagonal is None else jnp.where(diagonal, -scores, scores)
+
+
 def pair_gradient(scores, diagonal):
-    u = jnp.where(diagonal, -scores, scores)
-    sig = 1.0 / (1.0 + jnp.exp(-u))
-    return jnp.where(diagonal, -sig, sig)
-
-
-def pair_loss(scores, diagonal):
-    u = jnp.where(diagonal, -scores, scores)
-    return jnp.maximum(u, 0.0) + jnp.log1p(jnp.exp(-jnp.abs(u)))
+    sig = 1.0 / (1.0 + jnp.exp(-signed(scores, diagonal)))
+    return signed(sig, diagonal)
+
+
+def pair_terms(scores, diagonal):
+    u = signed(scores, diagonal)
+    e = jnp.exp(-jnp.abs(u))
+    d = 1.0 + e
+    r = 1.0 / d
+    return signed(jnp.where(u >= 0, r, e * r), diagonal), jnp.maximum(u, 0.0), d
 
 
 def kernel(
@@ -74,7 +80,9 @@
     hot,
     hot_t,
     g2,
-    g1,
+    own2,
+    lsum,
+    lprod,
     tsum,
     tgrad,
     tswap,
@@ -91,7 +99,7 @@
     h = lax.axis_index("shard")
     zh, y = lax.div(g, 4), lax.rem(g, 4)
     x, w = lax.div(h, 4), lax.rem(h, 4)
-    za, zb = lax.div(zh, 2), lax.rem(zh, 2)
+    zb = lax.rem(zh, 2)
     zl, b = lax.div(w, 2), lax.rem(w, 2)
     on = zb == b
     off = zb != b
@@ -110,10 +118,17 @@
     up = (jnp.where(on, ring(zh, 2), ring(zh, 1)) * 4 + y, jnp.where(on, h, flipped))
     down = (ring(zh, 3) * 4 + y, flipped)
 
-    def partner(step):
-        z = jnp.where(on, zh, za * 2 + 1 - zb)
-        c = jnp.where(on, b, 1 - b)
-        return (z * 4 + y, x * 4 + (1 - zl if step else zl) * 2 + c)
+    def home(step):
+        to = 1 - zl if step else zl
+        z = jnp.where(on, zh, ring(zh, jnp.where(to == 0, 1, 3)))
+        return (z * 4 + y, x * 4 + to * 2 + jnp.where(on, b, 1 - b))
+
+    def source(step):
+        z = jnp.where(on, zh, ring(zh, jnp.where(zl == 0, 3, 1)))
+        return (z * 4 + y, x * 4 + (1 - zl if step else zl) * 2 + jnp.where(on, b, 1 - b))
+
+    def text_z(core_bit):
+        return jnp.where(zb == core_bit, zh, ring(zh, jnp.where(zl == 0, 3, 1)))
 
     made = []
     local = []
@@ -151,16 +166,16 @@
         pl.semaphore_signal(barrier, inc=1, device_id=device, device_id_type=pl.DeviceIdType.MESH)
 
     partners = [at_x(s) for s in (1, 2, 3)] + [at_y(s) for s in (1, 3)]
-    partners += [core, up, partner(1)]
+    partners += [core, up, home(1), source(1)]
     for device in partners:
         greet(device)
 
     @pl.when(off)
     def _():
-        for device in (down, partner(0)):
+        for device in (down, home(0), source(0)):
             greet(device)
 
-    pl.semaphore_wait(barrier, len(partners) + jnp.where(on, 0, 2))
+    pl.semaphore_wait(barrier, len(partners) + jnp.where(on, 0, 3))
 
     id_copies = [send(ids_ref.at[ring(x, s)], idr.at[x], at_x(s)) for s in (2, 1, 3)]
     id_own = move(ids_ref.at[x], idr.at[x])
@@ -218,7 +233,8 @@
         for s in range(4):
             table = (idr[s, o : o + 1, :] == image_rows).astype(F32)
             hot[o, :, s * SLOT : (s + 1) * SLOT] = table.astype(BF16)
-            hot_t[o, s * SLOT : (s + 1) * SLOT, :] = table.T.astype(BF16)
+            table = (ids_ref[s, o : o + 1, :] == image_rows).astype(F32)
+            hot_t[s * 4 + o] = table.T.astype(BF16)
 
     up_copy.wait_recv()
 
@@ -238,6 +254,9 @@
     def _():
         for copy in far:
             copy.copy.start()
+
+    own2[:ROWS, :] = imgs[rows(near_slot(y)), :]
+    own2[ROWS:, :] = imgs[rows(far_slot(y)), :]
 
     p_copies = []
 
@@ -260,8 +279,8 @@
             psend[t, :, span] = (sums[t] + prsib[t, :, span].astype(F32)).astype(BF16)
         p_copies.append(
             [
-                send(psend.at[1 - zl, :, span], prec.at[1, :, span], partner(1)),
-                send(psend.at[zl, :, span], prec.at[0, :, span], partner(0), when=off),
+                send(psend.at[1 - zl, :, span], prec.at[1, :, span], home(1)),
+                send(psend.at[zl, :, span], prec.at[0, :, span], home(0), when=off),
             ]
         )
 
@@ -303,16 +322,17 @@
         copy.wait_recv()
     t_swaps[0].wait_recv()
     both = pl.ds(pl.multiple_of(y * 2 * ROWS, 128), 2 * ROWS)
-    for k in range(8):
-        scores = lax.dot_general(
-            txts[both, :], imgs[rows(first + k), :], nt, preferred_element_type=F32
-        )
-        image_z = z_far if k // 4 else z_near
-        for t in range(2):
-            same = (y == k % 4) & (image_z == za * 2 + t)
-            block = slice(t * ROWS, (t + 1) * ROWS)
-            grad = pair_gradient(mult * scores[block] + offset, diagonal(same))
-            g2[block, k * ROWS : (k + 1) * ROWS] = grad.astype(BF16)
+    for step in (0, 3, 1, 2):
+        for far_group, image_z in ((0, z_near), (1, z_far)):
+            slot = far_group * 4 + ring(y, step)
+            scores = lax.dot_general(
+                txts[both, :], imgs[rows(first + slot), :], nt, preferred_element_type=F32
+            )
+            for t in range(2):
+                block = slice(t * ROWS, (t + 1) * ROWS)
+                mask = None if step else diagonal(image_z == text_z(t))
+                grad = pair_gradient(mult * scores[block] + offset, mask)
+                g2[block, rows(slot)] = grad.astype(BF16)
     parts = (slice(0, 512), slice(512, 1024), slice(1024, D))
     g_swaps = []
     for span in parts:
@@ -338,71 +358,133 @@
         src = tswap.at[2, :, span]
         s_copies.append(
             [
-                send(src, sc.at[zb * 2 + zl, :, span], partner(1)),
-                send(src, sc.at[zb * 2 + zl, :, span], partner(0), when=off),
+                send(src, sc.at[x, zb * 2 + zl, :, span], source(1)),
+                send(src, sc.at[x, zb * 2 + zl, :, span], source(0), when=off),
             ]
         )
 
         @pl.when(on)
         def _():
-            sc[zb * 2 + zl, :, span] = tswap[2, :, span]
-
-    out_copies, out_own = [], []
-    t_halves = []
-    for j, span in enumerate(OUT):
+            sc[x, zb * 2 + zl, :, span] = tswap[2, :, span]
+
+    x_near = {}
+    x_far = {}
+    handed = {j: [] for j in range(len(OUT))}
+    out_own = []
+
+    def held(step, j, owner=None):
+        if owner is None:
+            return sc.at[ring(x, step), pl.ds(b * 2, 2), :, OUT[j]]
+        return sc.at[ring(x, step), b * 2 + owner, :, OUT[j]]
+
+    def hand(step, j):
+        src = held(step, j)
+        handed[j].append(send(src, src, core))
+
+    def start_x(j):
         for copy in s_copies[j]:
             copy.wait_recv()
-        src = sc.at[pl.ds(b * 2, 2), :, span]
-        send(src, src, core).wait_recv()
-        for s in (2, 1, 3, 0):
+        src = held(0, j)
+        x_near[j] = [send(src, src, at_x(s)) for s in (1, 3)]
+        hand(0, j)
+
+    def pass_x(j):
+        x_far[j] = []
+        for copy, step, owner in zip(x_near[j], (3, 1), (0, 1)):
+            copy.wait_recv()
+            src = held(step, j, owner)
+            x_far[j].append(send(src, src, at_x(4 - step)))
+            hand(step, j)
+
+    def last_x(j):
+        for copy in x_far[j]:
+            copy.wait_recv()
+        hand(2, j)
+
+    def write(j):
+        span = OUT[j]
+        for copy in handed[j]:
+            copy.wait_recv()
+        for s in range(4):
             for o in range(4):
-                xr[ring(x, s), o * SLOT : (o + 1) * SLOT, span] = jnp.dot(
-                    hot_t[o, pl.ds(pl.multiple_of(ring(x, s) * SLOT, SLOT), SLOT), :],
-                    sc[o % 2 * 2 + o // 2, :, span],
+                xr[s, o * SLOT : (o + 1) * SLOT, span] = jnp.dot(
+                    hot_t[s * 4 + o],
+                    sc[s, o % 2 * 2 + o // 2, :, span],
                     preferred_element_type=F32,
                 ).astype(BF16)
-            src = xr.at[ring(x, s), :, span]
-            dst = gcap_ref.at[piece(x), span]
-            if s:
-                out_copies.append(send(src, dst, at_x(s)))
-            else:
-                out_own.append(move(src, dst))
-        if j == 1:
-            t_halves = [pass_y(txts, text_slot, t_copies, step) for step in (3, 1)]
-            for step in (3, 1):
-                src = txts.at[rows(text_slot(ring(y, step)))]
-                t_swaps.append(send(src, src, core))
-
+        out_own.append(move(xr.at[:, :, span], gcap_ref.at[:, :, span]))
+
+    i_copies = []
+
+    def image_pairs(step):
+        column = ring(y, step) * 2 * ROWS
+        texts = pl.ds(pl.multiple_of(column, 128), 2 * ROWS)
+        scores = lax.dot_general(own2[...], txts[texts, :], nt, preferred_element_type=F32)
+        for n, image_z in ((0, z_near), (1, z_far)):
+            block = slice(n * ROWS, (n + 1) * ROWS)
+            relu, prod = (lsum[block], lprod[block]) if step else (0.0, 1.0)
+            for t in range(2):
+                mask = None if step else diagonal(image_z == text_z(t))
+                part = mult * scores[block, t * ROWS : (t + 1) * ROWS] + offset
+                grad, positive, d = pair_terms(part, mask)
+                relu += positive[:, :128] + positive[:, 128:]
+                prod *= d[:, :128] * d[:, 128:]
+                at = pl.ds(pl.multiple_of(column + t * ROWS, 128), ROWS)
+                g2[block, at] = grad.astype(BF16)
+            lsum[block] = relu
+            lprod[block] = prod
+
+    def image_grads(span):
+        part = mult * jnp.dot(g2[...], txts[:, span], preferred_element_type=F32)
+        for n, device, when in ((1, up, None), (0, down, off)):
+            gsend[n, :, span] = part[n * ROWS : (n + 1) * ROWS].astype(BF16)
+            i_copies.append(send(gsend.at[n, :, span], grecv.at[n, :, span], device, when))
+
+    def image_losses():
+        for n, device, when in ((1, up, None), (0, down, off)):
+            block = slice(n * ROWS, (n + 1) * ROWS)
+            lsend[n] = lsum[block] + jnp.log(lprod[block])
+            i_copies.append(send(lsend.at[n], lrecv.at[n], device, when))
+
+    start_x(0)
+    t_halves = [pass_y(txts, text_slot, t_copies, step) for step in (3, 1)]
+    for step in (3, 1):
+        src = txts.at[rows(text_slot(ring(y, step)))]
+        t_swaps.append(send(src, src, core))
+    image_pairs(0)
+    pass_x(0)
+    t_swaps[1].wait_recv()
+    image_pairs(3)
+    start_x(1)
+    t_swaps[2].wait_recv()
+    image_pairs(1)
     for copy in t_halves:
         copy.wait_recv()
     src = txts.at[rows(text_slot(ring(y, 2)))]
     t_swaps.append(send(src, src, core))
-    for copy in t_swaps[1:]:
-        copy.wait_recv()
-    i_copies = []
-    for far in (1, 0):
-        image_z = z_far if far else z_near
-        loss_part = jnp.zeros((ROWS, 128), F32)
-        for k in range(8):
-            scores = lax.dot_general(
-                imgs[rows(first + far * 4 + y), :],
-                txts[k * ROWS : (k + 1) * ROWS, :],
-                nt,
-                preferred_element_type=F32,
-            )
-            same = (y == k // 2) & (image_z == za * 2 + k % 2)
-            scores = mult * scores + offset
-            grad = pair_gradient(scores, diagonal(same))
-            losses = pair_loss(scores, diagonal(same))
-            loss_part += losses[:, :128] + losses[:, 128:]
-            g1[:, k * ROWS : (k + 1) * ROWS] = grad.astype(BF16)
-        gsend[far] = (
-            mult * jnp.dot(g1[...], txts[...], preferred_element_type=F32)
-        ).astype(BF16)
-        lsend[far] = loss_part
-        device, when = (up, None) if far else (down, off)
-        i_copies.append(send(gsend.at[far], grecv.at[far], device, when))
-        i_copies.append(send(lsend.at[far], lrecv.at[far], device, when))
+    start_x(2)
+    pass_x(1)
+    t_swaps[3].wait_recv()
+    image_pairs(2)
+    image_grads(slice(0, 384))
+    start_x(3)
+    pass_x(2)
+    last_x(0)
+    image_grads(slice(384, 768))
+    start_x(4)
+    write(0)
+    image_grads(slice(768, D))
+    image_losses()
+    pass_x(3)
+    last_x(1)
+    write(1)
+    pass_x(4)
+    last_x(2)
+    write(2)
+    last_x(3)
+    write(3)
+    last_x(4)
+    write(4)
 
     @pl.when(on)
     def _():
@@ -421,8 +503,6 @@
     along = jnp.sum(unit * total, axis=-1, keepdims=True)
     gimg_ref[...] = ((total - unit * along) / pic_norm).astype(BF16)
 
-    for copy in out_copies:
-        copy.wait_recv()
     for copy in out_own:
         copy.wait()
     for copy in made:
@@ -430,7 +510,8 @@
 
 
 def hand_over(loss_ref, gimg_ref, gcap_ref, loss_out, gimg_out, gcap_out, held, in_sem, out_sem):
-    pieces = [(gcap_ref, gcap_out, i * ROWS) for i in range(8)] + [(gimg_ref, gimg_out, 0)]
+    pieces = [(gcap_ref.at[i // 2], gcap_out.at[i // 2], i % 2 * ROWS) for i in range(8)]
+    pieces.append((gimg_ref, gimg_out, 0))
     ins, outs = [], []
     for i, (src, dst, row) in enumerate(pieces):
         part = pl.ds(row, ROWS)
@@ -454,7 +535,7 @@
         out_shape=(
             jax.ShapeDtypeStruct((1, ROWS), F32),
             jax.ShapeDtypeStruct((ROWS, D), BF16),
-            jax.ShapeDtypeStruct((16 * SLOT, D), BF16),
+            jax.ShapeDtypeStruct((4, 4 * SLOT, D), BF16),
         ),
         in_specs=[smem, smem, vmem, vmem, anywhere],
         out_specs=(vmem, vmem, anywhere),
@@ -468,13 +549,15 @@
             pltpu.VMEM((2, ROWS, D), BF16),
             pltpu.VMEM((2, ROWS, D), BF16),
             pltpu.VMEM((4, ROWS, 4 * SLOT), BF16),
-            pltpu.VMEM((4, 4 * SLOT, ROWS), BF16),
+            pltpu.VMEM((16, SLOT, ROWS), BF16),
             pltpu.VMEM((2 * ROWS, 8 * ROWS), BF16),
-            pltpu.VMEM((ROWS, 8 * ROWS), BF16),
+            pltpu.VMEM((2 * ROWS, D), BF16),
+            pltpu.VMEM((2 * ROWS, 128), F32),
+            pltpu.VMEM((2 * ROWS, 128), F32),
             pltpu.VMEM((ROWS, D), F32),
             pltpu.VMEM((2 * ROWS, D), F32),
             pltpu.VMEM((3, ROWS, D), BF16),
-            pltpu.VMEM((4, ROWS, D), BF16),
+            pltpu.VMEM((4, 4, ROWS, D), BF16),
             pltpu.VMEM((2, ROWS, D), BF16),
             pltpu.VMEM((2, ROWS, D), BF16),
             pltpu.VMEM((2, ROWS, 128), F32),
@@ -510,7 +593,7 @@
         compiler_params=pltpu.CompilerParams(vmem_limit_bytes=60 * 1024 * 1024),
         name="hand_over",
     )(*parts)
-    return loss.reshape(ROWS), grad_images, grad_captions
+    return loss.reshape(ROWS), grad_images, grad_captions.reshape(16 * SLOT, D)
 
 
 def solution(mesh):

time: 162 us -> 146 us (0.901)
  Pallas kernels: 160 us -> 143 us
    pallas_call x1, Pallas kernels: 154 us -> 137 us  [body(): pl.pallas_call(kernel, out_shape=(jax.ShapeDtypeStruct((1, ROWS), F32), j...]
where the time goes in v3:
time: 146 us; the launch traced here: 145 us
  Pallas kernels  143 us (98%)
  between operations  2.09 us (1%)
    pallas_call x1, Pallas kernels, body(): pl.pallas_call(kernel, out_shape=(jax.ShapeDtypeStruct((1, ROWS), F32), j...  137 us
    pallas_call x1, Pallas kernels, body(): pl.pallas_call(hand_over, out_shape=tuple((jax.ShapeDtypeStruct(p.shape,...  5.97 us

profile of v3, /device:TPU:33, one launch (start us, length us, event | category | flops | bytes accessed | tf_op | source)
XLA Modules:
  0.0 145.3 jit_solution(17303830232309508452)
XLA Ops:
  1.9 137.3 %pooled_sigmoid_loss.1 = (f32[1,256]{1,0:T(1,128)}, bf16[256,1152]{1,0:T(8,128)(2,1)}, bf16[4,512,1152]{2,1,0:T(8,128)(2,1)}) custom-call(f32[1]{0:T(128)} %bitcast.5.mult_ref, f32[1]{0:T(128)} %bitcast.6.off_ref, s32[4,4,128]{2,1,0:T(4,128)} %bitcast.8, bf16[256,1152]{1,0:T(8,128)(2,1)} %img_ref.1, bf16[2048,1152]{1,0:T(8,128)(2,1)} %cap_ref.1), custom_call_target="tpu_custom_call" | custom-call | flops 12999999488 | bytes 12000000 | tf_op jit(solution)/shard_map/pooled_sigmoid_loss/pallas_call | solution.py:533
  139.2 6.0 %hand_over.1 = (f32[1,256]{1,0:T(1,128)}, bf16[256,1152]{1,0:T(8,128)(2,1)}, bf16[4,512,1152]{2,1,0:T(8,128)(2,1)}) custom-call(f32[1,256]{1,0:T(1,128)} %get-tuple-element.9.loss_ref, bf16[256,1152]{1,0:T(8,128)(2,1)} %get-tuple-element.10.gimg_ref, bf16[4,512,1152]{2,1,0:T(8,128)(2,1)} %get-tuple-element.11.gcap_ref), custom_call_target="tpu_custom_call" | custom-call | tf_op jit(solution)/shard_map/hand_over/pallas_call | solution.py:583

commit v4 on v3

--- a/solution.py
+++ b/solution.py
@@ -81,6 +81,9 @@
     hot_t,
     g2,
     own2,
+    iunit,
+    along_sum,
+    along_got,
     lsum,
     lprod,
     tsum,
@@ -191,7 +194,9 @@
 
     pics = img_ref[...].astype(F32)
     pic_norm = jnp.sqrt(jnp.sum(pics * pics, axis=-1, keepdims=True) + EPS)
-    imgs[rows(y), :] = (pics / pic_norm).astype(BF16)
+    pic_scale = 1.0 / pic_norm
+    iunit[...] = pics * pic_scale
+    imgs[rows(y), :] = iunit[...].astype(BF16)
     first = jnp.where(on, 0, 4)
     z_near = jnp.where(on, zh, ring(zh, 3))
     z_far = jnp.where(on, ring(zh, 2), ring(zh, 1))
@@ -322,6 +327,7 @@
         copy.wait_recv()
     t_swaps[0].wait_recv()
     both = pl.ds(pl.multiple_of(y * 2 * ROWS, 128), 2 * ROWS)
+    along_parts = [jnp.zeros((ROWS, 128), F32)] * 2
     for step in (0, 3, 1, 2):
         for far_group, image_z in ((0, z_near), (1, z_far)):
             slot = far_group * 4 + ring(y, step)
@@ -331,11 +337,19 @@
             for t in range(2):
                 block = slice(t * ROWS, (t + 1) * ROWS)
                 mask = None if step else diagonal(image_z == text_z(t))
-                grad = pair_gradient(mult * scores[block] + offset, mask)
-                g2[block, rows(slot)] = grad.astype(BF16)
-    parts = (slice(0, 512), slice(512, 1024), slice(1024, D))
-    g_swaps = []
-    for span in parts:
+                part = mult * scores[block]
+                grad = pair_gradient(part + offset, mask).astype(BF16)
+                g2[block, rows(slot)] = grad
+                part = grad.astype(F32) * part
+                along_parts[t] += part[:, :128] + part[:, 128:]
+    for t in range(2):
+        along_sum[t] = along_parts[t]
+    along_swap = send(along_sum.at[1 - b], along_got, core)
+
+    g_swaps, s_copies = [], []
+
+    def text_grad(j):
+        span = OUT[j]
         tgrad[:, span] = mult * jnp.dot(
             g2[...],
             imgs[pl.ds(pl.multiple_of(first * ROWS, 128), 8 * ROWS), span],
@@ -344,17 +358,11 @@
         tswap[0, :, span] = tgrad[rows(1 - b), span].astype(BF16)
         g_swaps.append(send(tswap.at[0, :, span], tswap.at[1, :, span], core))
 
-    along = jnp.zeros((ROWS, 1), F32)
-    for copy, span in zip(g_swaps, parts):
-        copy.wait_recv()
+    def scale(j):
+        span = OUT[j]
+        g_swaps[j].wait_recv()
         total = tgrad[rows(b), span] + tswap[1, :, span].astype(F32)
-        tgrad[rows(b), span] = total
-        along += jnp.sum(tsum[:, span] * total, axis=-1, keepdims=True)
-    s_copies = []
-    for span in OUT:
-        tswap[2, :, span] = (
-            (tgrad[rows(b), span] - tsum[:, span] * along) * text_scale
-        ).astype(BF16)
+        tswap[2, :, span] = ((total - tsum[:, span] * along) * text_scale).astype(BF16)
         src = tswap.at[2, :, span]
         s_copies.append(
             [
@@ -366,6 +374,19 @@
         @pl.when(on)
         def _():
             sc[x, zb * 2 + zl, :, span] = tswap[2, :, span]
+
+    text_grad(0)
+    text_grad(1)
+    along_swap.wait_recv()
+    along = jnp.sum(along_sum[b] + along_got[...], axis=-1, keepdims=True)
+    scale(0)
+    text_grad(2)
+    scale(1)
+    text_grad(3)
+    scale(2)
+    text_grad(4)
+    scale(3)
+    scale(4)
 
     x_near = {}
     x_far = {}
@@ -497,11 +518,9 @@
     losses = lrecv[0] + lrecv[1]
     loss_ref[...] = jnp.sum(losses.T, axis=0, keepdims=True) / TOTAL
     total = grecv[0].astype(F32) + grecv[1].astype(F32)
-    pics = img_ref[...].astype(F32)
-    pic_norm = jnp.sqrt(jnp.sum(pics * pics, axis=-1, keepdims=True) + EPS)
-    unit = pics / pic_norm
+    unit = iunit[...]
     along = jnp.sum(unit * total, axis=-1, keepdims=True)
-    gimg_ref[...] = ((total - unit * along) / pic_norm).astype(BF16)
+    gimg_ref[...] = ((total - unit * along) * pic_scale).astype(BF16)
 
     for copy in out_own:
         copy.wait()
@@ -552,6 +571,9 @@
             pltpu.VMEM((16, SLOT, ROWS), BF16),
             pltpu.VMEM((2 * ROWS, 8 * ROWS), BF16),
             pltpu.VMEM((2 * ROWS, D), BF16),
+            pltpu.VMEM((ROWS, D), F32),
+            pltpu.VMEM((2, ROWS, 128), F32),
+            pltpu.VMEM((ROWS, 128), F32),
             pltpu.VMEM((2 * ROWS, 128), F32),
             pltpu.VMEM((2 * ROWS, 128), F32),
             pltpu.VMEM((ROWS, D), F32),

time: 146 us -> 146 us (level)
  no operation moved by 1% of the time
where the time goes in v4:
time: 146 us
  Pallas kernels  144 us (99%)
  between operations  2.09 us (1%)
    pallas_call x1, Pallas kernels, body(): pl.pallas_call(kernel, out_shape=(jax.ShapeDtypeStruct((1, ROWS), F32), j...  138 us
    pallas_call x1, Pallas kernels, body(): pl.pallas_call(hand_over, out_shape=tuple((jax.ShapeDtypeStruct(p.shape,...  5.97 us

profile of v4, /device:TPU:33, one launch (start us, length us, event | category | flops | bytes accessed | tf_op | source)
XLA Modules:
  0.0 145.9 jit_solution(3202304675955515386)
XLA Ops:
  1.9 137.8 %pooled_sigmoid_loss.1 = (f32[1,256]{1,0:T(1,128)}, bf16[256,1152]{1,0:T(8,128)(2,1)}, bf16[4,512,1152]{2,1,0:T(8,128)(2,1)}) custom-call(f32[1]{0:T(128)} %bitcast.5.mult_ref, f32[1]{0:T(128)} %bitcast.6.off_ref, s32[4,4,128]{2,1,0:T(4,128)} %bitcast.8, bf16[256,1152]{1,0:T(8,128)(2,1)} %img_ref.1, bf16[2048,1152]{1,0:T(8,128)(2,1)} %cap_ref.1), custom_call_target="tpu_custom_call" | custom-call | flops 12999999488 | bytes 12000000 | tf_op jit(solution)/shard_map/pooled_sigmoid_loss/pallas_call | solution.py:552
  139.8 6.0 %hand_over.1 = (f32[1,256]{1,0:T(1,128)}, bf16[256,1152]{1,0:T(8,128)(2,1)}, bf16[4,512,1152]{2,1,0:T(8,128)(2,1)}) custom-call(f32[1,256]{1,0:T(1,128)} %get-tuple-element.9.loss_ref, bf16[256,1152]{1,0:T(8,128)(2,1)} %get-tuple-element.10.gimg_ref, bf16[4,512,1152]{2,1,0:T(8,128)(2,1)} %get-tuple-element.11.gcap_ref), custom_call_target="tpu_custom_call" | custom-call | tf_op jit(solution)/shard_map/hand_over/pallas_call | solution.py:605
